TPU v7x, 32 devices: a whole 2x2x4 slice. The times are simulated.
32 devices in a mesh: dp: 2 (over x), expert: 4 (over y, core), mp: 4 (over z).
Axes of the slice: x: 2, y: 2, z: 4, core: 2. Of those that a mesh axis runs over, the one named last changes fastest.
Arguments:
- tokens: bfloat16 [128, 3072], P('dp'), may hold values from -6 to 6
- expert_ids: int32 [128, 2], P('dp'), may hold values from 0 to 3, all different within a row; in each aligned block of 64 rows (0 to 63, 64 to 127, ...) at most 64 rows name the same one
- gate_values: float32 [128, 2], P('dp'), may hold values from 0.2 to 1
- targets: int32 [128], P('dp'), may hold values from 0 to 32767
- w_gate: bfloat16 [4, 3072, 4, 2048], P('expert', None, 'mp', 'dp'), may hold values from -0.109375 to 0.109375
- w_up: bfloat16 [4, 3072, 4, 2048], P('expert', None, 'mp', 'dp'), may hold values from -0.109375 to 0.109375
- w_down: bfloat16 [4, 4, 2048, 3072], P('expert', 'mp', None, 'dp'), may hold values from -0.0625 to 0.0625
- norm_gain: float32 [3072], replicated, may hold values from 0.1 to 1.9
- lens_head: bfloat16 [3072, 32768], P('dp', ('expert', 'mp')), may hold values from -120 to 120
Outputs:
- mixed: bfloat16 [128, 3072], P('dp')
- log_probs: float32 [128], P('dp')
Inputs may be any that keep to these rules, and one draw needn't show every extreme that they name: `expert_ids`: each row names two different experts; in each aligned block of 64 rows no expert is named by more than 64 rows, a bound that some block reaches.
All inputs are finite; a program needn't handle non-finite values.
Results may differ from a plain program's by a relative error of at most 0.0041.
Values may be sent and summed in bfloat16 or wider, within the bound.
A program may use at most 128 MiB of HBM per device.

v0:
```python
import jax
import jax.numpy as jnp
from jax import lax
from jax.sharding import PartitionSpec as P


def per_device(
    tokens, expert_ids, gate_values, targets, w_gate, w_up, w_down, norm_gain, lens_head
):
    row_count = tokens.shape[0]
    feat_count = tokens.shape[1]
    owner = lax.axis_index("expert")
    capacity = min(row_count, 4 * row_count // lax.axis_size("expert"))
    matches = expert_ids == owner
    chosen = jnp.any(matches, axis=1)
    weights = jnp.sum(jnp.where(matches, gate_values, jnp.float32(0.0)), axis=1)
    position = jnp.cumsum(chosen.astype(jnp.int32)) - 1
    slot_ids = lax.broadcasted_iota(jnp.int32, (capacity, row_count), 0)
    placing = (slot_ids == position[None, :]) & chosen[None, :]
    picker = placing.astype(jnp.bfloat16)
    picked = jnp.dot(picker, tokens, preferred_element_type=jnp.float32).astype(jnp.bfloat16)
    gate_mat = w_gate.reshape(feat_count, -1)
    up_mat = w_up.reshape(feat_count, -1)
    down_mat = w_down.reshape(w_down.shape[2], w_down.shape[3])
    shard_part = lax.all_gather(picked, "dp", axis=0, tiled=True)
    gate_part = jnp.dot(shard_part, gate_mat, preferred_element_type=jnp.float32)
    up_part = jnp.dot(shard_part, up_mat, preferred_element_type=jnp.float32)
    hidden = (jax.nn.silu(gate_part) * up_part).astype(jnp.bfloat16)
    partial_value = jnp.dot(
        lax.all_gather(hidden, "dp", axis=1, tiled=True),
        down_mat,
        preferred_element_type=jnp.float32,
    )
    expert_out = lax.psum(partial_value, "mp").astype(jnp.bfloat16)
    returned = lax.all_to_all(expert_out, "dp", split_axis=0, concat_axis=1, tiled=True)
    spread_w = placing.astype(jnp.float32) * weights[None, :]
    contrib = lax.dot_general(
        spread_w,
        returned.astype(jnp.float32),
        (((0,), (0,)), ((), ())),
        precision=lax.Precision.HIGHEST,
    )
    summed = lax.psum(contrib, "expert")
    mixed = (tokens.astype(jnp.float32) + summed).astype(jnp.bfloat16)
    mixed_f = mixed.astype(jnp.float32)
    scale = lax.rsqrt(jnp.mean(mixed_f * mixed_f, axis=1, keepdims=True) + 1e-05)
    normed = (mixed_f * scale * norm_gain[None, :]).astype(jnp.bfloat16)
    vocab_cols = lens_head.shape[1]
    vocab_start = (
        lax.axis_index("expert") * lax.axis_size("mp") + lax.axis_index("mp")
    ) * vocab_cols
    logits = jnp.dot(
        normed,
        lax.all_gather(lens_head, "dp", axis=0, tiled=True),
        preferred_element_type=jnp.float32,
    )
    columns = vocab_start + lax.broadcasted_iota(jnp.int32, (1, vocab_cols), 1)
    target_hit = columns == targets[:, None]
    target_local = jnp.sum(jnp.where(target_hit, logits, jnp.float32(0.0)), axis=1)
    local_top = jnp.max(logits, axis=1)
    global_top = lax.pmax(local_top, ("expert", "mp"))
    local_total = jnp.sum(jnp.exp(logits - global_top[:, None]), axis=1)
    exp_total, target_logit = lax.psum((local_total, target_local), ("expert", "mp"))
    log_probs = target_logit - global_top - jnp.log(exp_total)
    return (mixed, log_probs)


def solution(mesh):
    in_specs = (
        P("dp", None),
        P("dp", None),
        P("dp", None),
        P("dp"),
        P("expert", None, "mp", "dp"),
        P("expert", None, "mp", "dp"),
        P("expert", "mp", None, "dp"),
        P(),
        P("dp", ("expert", "mp")),
    )
    out_specs = (P("dp", None), P("dp"))
    return jax.shard_map(
        per_device, mesh=mesh, in_specs=in_specs, out_specs=out_specs, check_vma=False
    )
```

profile of v0, /device:TPU:0, one launch (start us, length us, event | category | flops | bytes accessed | tf_op | source)
XLA Modules:
  0.0 313.7 jit_solution(13185323935273320964)
XLA Ops:
  8.0 0.7 fusion.31
  8.7 0.1 copy.14
  8.8 0.1 reduce-window.8
  8.9 0.1 add_reduce_fusion
  9.0 0.0 slice-start.2
  9.0 1.4 convolution_convert_fusion
  10.4 12.7 %all_gather.9 = bf16[128,3072]{1,0:T(8,128)(2,1)S(1)} all-gather(bf16[64,3072]{1,0:T(8,128)(2,1)S(1)} %convolution_convert_fusion), channel_id=1, replica_groups=mesh['dp'=2,'expert'=4,'mp'=4] {'dp'}, dimensions={0}, use_global_device_ids=true | all-gather | bytes 1179648 | tf_op jit(solution)/shard_map/all_gather | solution.py:25
  23.2 0.0 slice-start.3
  23.2 0.0 slice-start
  23.2 4.0 %fusion.4 = f32[128,1024]{1,0:T(8,128)S(1)} fusion(bf16[128,3072]{1,0:T(8,128)(2,1)S(1)} %all_gather.9, bf16[1,3072,1,1024]{3,1,2,0:T(8,128)(2,1)} %param.13), kind=kOutput, calls=%fused_computation.4 | convolution fusion | flops 805306368 | bytes 7602176 | tf_op jit(solution)/shard_map/dot_general | solution.py:26
  27.1 0.0 slice-done.2
  27.2 0.0 slice-done.3
  27.2 0.0 slice-start.1
  27.2 1.1 fusion.9
  28.3 8.2 %all_gather.10 = bf16[128,2048]{1,0:T(8,128)(2,1)S(1)} all-gather(bf16[128,1024]{1,0:T(8,128)(2,1)S(1)} %fusion.9), channel_id=1, replica_groups=mesh['dp'=2,'expert'=4,'mp'=4] {'dp'}, dimensions={1}, use_global_device_ids=true | all-gather | bytes 786432 | tf_op jit(solution)/shard_map/all_gather | solution.py:30
  36.4 0.0 slice-done
  36.4 0.0 slice-done.1
  36.4 0.0 copy-start.3
  36.4 0.0 copy-start.4
  36.5 1.0 fusion
  37.5 0.0 copy-start.1
  37.5 0.0 copy-start.2
  37.5 35.0 %all-reduce.5 = bf16[128,1536]{1,0:T(8,128)(2,1)} all-reduce(f32[128,1536]{1,0:T(8,128)S(1)} %fusion), channel_id=1, replica_groups=mesh['dp'=2,'expert'=4,'mp'=4] {'mp'}, use_global_device_ids=true, to_apply=%region_3.4 | all-reduce | flops 196608 | bytes 1179648 | tf_op jit(solution)/shard_map/psum | solution.py:34
  72.5 3.5 %all-to-all-start = ((bf16[2,64,1536]{2,1,0:T(8,128)(2,1)}), bf16[2,64,1536]{2,1,0:T(8,128)(2,1)S(1)}, u32[]{:S(2)}, u32[]{:S(2)}) async-start(bf16[2,64,1536]{2,1,0:T(8,128)(2,1)} %bitcast.4), calls=%async_computation | async-start | bytes 786432 | tf_op jit(solution)/shard_map/all_to_all | solution.py:35
  76.0 0.0 all-reduce.4.cloned.1.call-start
  76.0 0.0 copy-done.3
  76.1 0.0 copy-done.4
  76.1 5.8 %all-to-all-done = bf16[2,64,1536]{2,1,0:T(8,128)(2,1)S(1)} async-done(((bf16[2,64,1536]{2,1,0:T(8,128)(2,1)}), bf16[2,64,1536]{2,1,0:T(8,128)(2,1)S(1)}, u32[]{:S(2)}, u32[]{:S(2)}) %all-to-all-start) | async-done | bytes 393248 | tf_op jit(solution)/shard_map/all_to_all | solution.py:35
  81.9 1.4 fusion.19
  83.3 0.0 all-reduce.4.cloned.1.call-update
  83.3 0.0 all-gather.2.cloned.1.call-start
  83.4 0.5 all-gather.2.cloned.1.call-update
  83.9 32.0 %all-reduce.4.cloned.1.call-done = f32[64,3072]{1,0:T(8,128)} async-done(((f32[64,3072]{1,0:T(8,128)}), f32[64,3072]{1,0:T(8,128)}) %all-reduce.4.cloned.1.call-update) | async-done | bytes 786448 | tf_op jit(solution)/shard_map/psum | solution.py:43
  116.0 0.0 copy-done.1
  116.0 1.3 fusion.12
  117.3 0.0 copy-start
  117.3 118.1 %all-gather.2.cloned.1.call-done = bf16[3072,2048]{1,0:T(8,128)(2,1)} async-done(((bf16[1536,2048]{1,0:T(8,128)(2,1)}), bf16[3072,2048]{1,0:T(8,128)(2,1)}) %all-gather.2.cloned.1.call-update) | async-done | bytes 12582928 | tf_op jit(solution)/shard_map/all_gather | solution.py:54
  235.5 0.0 copy-done.2
  235.5 0.0 copy-start.5
  235.5 7.0 %fusion.32 = (f32[64]{0:T(128)S(1)}, f32[64,2048]{1,0:T(8,128)S(1)}) fusion(bf16[3072,2048]{1,0:T(8,128)(2,1)} %all-gather.2.cloned.1.call-done, bf16[64,3072]{1,0:T(8,128)(2,1)S(1)} %get-tuple-element.7, f32[3072]{0:T(1024)S(1)} %copy-done.2, f32[64]{0:T(128)S(1)} %add_rsqrt_fusion), kind=kOutput, calls=%fused_computation.39 | convolution fusion | flops 806223808 | bytes 13513216 | tf_op jit(solution)/shard_map/dot_general | solution.py:52
  242.5 0.0 copy-done
  242.5 33.2 %pmax.7 = f32[64]{0:T(128)S(1)} all-reduce(f32[64]{0:T(128)S(1)} %get-tuple-element.8), channel_id=1, replica_groups=mesh['dp'=2,'expert'=4,'mp'=4] {'expert','mp'}, use_global_device_ids=true, to_apply=%region_9.10 | all-reduce | flops 64 | bytes 512 | tf_op jit(solution)/shard_map/pmax | solution.py:61
  275.8 0.0 copy-done.5
  275.8 0.3 select_reduce_fusion
  276.0 29.7 %all-reduce = (f32[64]{0:T(128)S(1)}, f32[64]{0:T(128)S(1)}) all-reduce(f32[64]{0:T(128)S(1)} %get-tuple-element.3, f32[64]{0:T(128)S(1)} %get-tuple-element.2), channel_id=1, replica_groups=mesh['dp'=2,'expert'=4,'mp'=4] {'expert','mp'}, use_global_device_ids=true, to_apply=%region_11.12 | all-reduce | flops 128 | bytes 1024 | tf_op jit(solution)/shard_map/psum | solution.py:63
  305.7 0.5 log_subtract_fusion
  (7 shorter events, 0.1 us)
Async XLA Ops:
  9.0 18.1 %slice-start.2 = ((s8[6291456]{0:T(1024)(128)(4,1)}), s8[4194304]{0:T(1024)(128)(4,1)S(1)}, s32[]{:S(2)}) async-start(s8[6291456]{0:T(1024)(128)(4,1)} %bitcast.29), calls=%async_computation.5 | async-start | bytes 8388608
  23.2 4.0 %slice-start.3 = ((s8[6291456]{0:T(1024)(128)(4,1)}), s8[2097152]{0:T(1024)(128)(4,1)S(1)}, s32[]{:S(2)}) async-start(s8[6291456]{0:T(1024)(128)(4,1)} %bitcast.29), calls=%async_computation.6 | async-start | bytes 4194304
  23.2 13.3 %slice-start = ((s8[6291456]{0:T(1024)(128)(4,1)}), s8[4194304]{0:T(1024)(128)(4,1)S(1)}, s32[]{:S(2)}) async-start(s8[6291456]{0:T(1024)(128)(4,1)} %bitcast.25), calls=%async_computation.3 | async-start | bytes 8388608
  27.2 9.3 %slice-start.1 = ((s8[6291456]{0:T(1024)(128)(4,1)}), s8[2097152]{0:T(1024)(128)(4,1)S(1)}, s32[]{:S(2)}) async-start(s8[6291456]{0:T(1024)(128)(4,1)} %bitcast.25), calls=%async_computation.4 | async-start | bytes 4194304
  36.4 39.6 %copy-start.3 = (s32[64,2]{0,1:T(2,128)S(1)}, s32[64,2]{0,1:T(2,128)}, u32[]{:S(2)}) copy-start(s32[64,2]{0,1:T(2,128)} %param.10) | copy-start | bytes 1540
  36.4 39.6 %copy-start.4 = (f32[64,2]{0,1:T(2,128)S(1)}, f32[64,2]{0,1:T(2,128)}, u32[]{:S(2)}) copy-start(f32[64,2]{0,1:T(2,128)} %param.11) | copy-start | bytes 1540
  37.5 78.5 %copy-start.1 = (bf16[64,3072]{1,0:T(8,128)(2,1)S(1)}, bf16[64,3072]{1,0:T(8,128)(2,1)}, u32[]{:S(2)}) copy-start(bf16[64,3072]{1,0:T(8,128)(2,1)} %param.9) | copy-start | bytes 1179652
  37.5 198.0 %copy-start.2 = (f32[3072]{0:T(1024)S(1)}, f32[3072]{0:T(1024)}, u32[]{:S(2)}) copy-start(f32[3072]{0:T(1024)} %param.16) | copy-start | bytes 36868
  72.5 9.3 %all-to-all-start = ((bf16[2,64,1536]{2,1,0:T(8,128)(2,1)}), bf16[2,64,1536]{2,1,0:T(8,128)(2,1)S(1)}, u32[]{:S(2)}, u32[]{:S(2)}) async-start(bf16[2,64,1536]{2,1,0:T(8,128)(2,1)} %bitcast.4), calls=%async_computation | async-start | bytes 786432 | tf_op jit(solution)/shard_map/all_to_all | solution.py:35
  76.0 40.0 %all-reduce.4.cloned.1.call-start = ((), (), s32[]{:S(2)}) async-start(), calls=%async_computation.1 | async-start | bytes 1572864 | tf_op jit(solution)/shard_map/psum | solution.py:43
  83.3 152.1 %all-gather.2.cloned.1.call-start = ((), (), s32[]{:S(2)}) async-start(), calls=%async_computation.2 | async-start | bytes 18874368 | tf_op jit(solution)/shard_map/all_gather | solution.py:54
  117.3 125.2 %copy-start = (bf16[64,3072]{1,0:T(8,128)(2,1)}, bf16[64,3072]{1,0:T(8,128)(2,1)S(1)}, u32[]{:S(2)}) copy-start(bf16[64,3072]{1,0:T(8,128)(2,1)S(1)} %get-tuple-element.7) | copy-start | bytes 1179652
  235.5 40.3 %copy-start.5 = (s32[64]{0:T(128)S(1)}, s32[64]{0:T(128)}, u32[]{:S(2)}) copy-start(s32[64]{0:T(128)} %param.12) | copy-start | bytes 772
Sparse Core Ops, SparseCore 0:
  83.4 32.4 all-reduce.3
Sparse Core Ops, SparseCore 1:
  85.4 150.0 all-gather.1
where the time goes:
time: 314 us
  waiting for transfers between devices  156 us (50%)
  blocking collectives  119 us (38%)
  matrix products  15.9 us (5%)
  between operations  15.7 us (5%)
  starting transfers between devices  3.55 us (1%)
    all_gather x1, waiting for transfers between devices, per_device(): lax.all_gather(lens_head, 'dp', axis=0, tiled=True)  118 us
    psum x1, blocking collectives, per_device(): expert_out = lax.psum(partial_value, 'mp').astype(jnp.bfloat16)  35 us
    pmax x1, blocking collectives, per_device(): global_top = lax.pmax(local_top, ('expert', 'mp'))  33.2 us
    psum x1, waiting for transfers between devices, per_device(): summed = lax.psum(contrib, 'expert')  32 us
    psum x1, blocking collectives, per_device(): lax.psum((local_total, target_local), ('expert', 'mp'))  29.7 us
    all_gather x1, blocking collectives, per_device(): shard_part = lax.all_gather(picked, 'dp', axis=0, tiled=True)  12.7 us
    all_gather x1, blocking collectives, per_device(): lax.all_gather(hidden, 'dp', axis=1, tiled=True)  8.17 us
    dot_general x1, matrix products, per_device(): jnp.dot(normed, lax.all_gather(lens_head, 'dp', axis=0, tiled=True), pref...  7.05 us
  transfers between devices with their start and end apart: 3, of which 3 were waited for; matrix products, arithmetic and copies ran while one was open for 0% of the time, Pallas kernels for 0%

commit v1 on v0

--- a/solution.py
+++ b/solution.py
@@ -60,7 +60,7 @@
     local_top = jnp.max(logits, axis=1)
     global_top = lax.pmax(local_top, ("expert", "mp"))
     local_total = jnp.sum(jnp.exp(logits - global_top[:, None]), axis=1)
-    exp_total, target_logit = lax.psum((local_total, target_local), ("expert", "mp"))
+    exp_total, target_logit = lax.psum(lax.psum((local_total, target_local), "mp"), "expert")
     log_probs = target_logit - global_top - jnp.log(exp_total)
     return (mixed, log_probs)
 

time: 314 us -> 299 us (0.952)
  blocking collectives: 119 us -> 103 us
    psum x1 -> x2, blocking collectives: 29.7 us -> 14.3 us  [the longest x1 8.37 us: per_device(): lax.psum((local_total, target_local), 'mp')]
where the time goes in v1:
time: 299 us; the launch traced here: 298 us
  waiting for transfers between devices  156 us (52%)
  blocking collectives  103 us (34%)
  matrix products  15.9 us (5%)
  between operations  15.7 us (5%)
  starting transfers between devices  3.55 us (1%)
  other arithmetic  3.1 us (1%)
    all_gather x1, waiting for transfers between devices, per_device(): lax.all_gather(lens_head, 'dp', axis=0, tiled=True)  118 us
    psum x1, blocking collectives, per_device(): expert_out = lax.psum(partial_value, 'mp').astype(jnp.bfloat16)  35 us
    pmax x1, blocking collectives, per_device(): global_top = lax.pmax(local_top, ('expert', 'mp'))  33.2 us
    psum x1, waiting for transfers between devices, per_device(): summed = lax.psum(contrib, 'expert')  32 us
    all_gather x1, blocking collectives, per_device(): shard_part = lax.all_gather(picked, 'dp', axis=0, tiled=True)  12.7 us
    psum x1, blocking collectives, per_device(): lax.psum((local_total, target_local), 'mp')  8.37 us
    all_gather x1, blocking collectives, per_device(): lax.all_gather(hidden, 'dp', axis=1, tiled=True)  8.17 us
    dot_general x1, matrix products, per_device(): jnp.dot(normed, lax.all_gather(lens_head, 'dp', axis=0, tiled=True), pref...  7.05 us
  transfers between devices with their start and end apart: 3, of which 3 were waited for; matrix products, arithmetic and copies ran while one was open for 0% of the time, Pallas kernels for 0%

profile of v1, /device:TPU:0, one launch (start us, length us, event | category | flops | bytes accessed | tf_op | source)
XLA Modules:
  0.0 298.3 jit_solution(2949842133417568853)
XLA Ops:
  8.0 0.7 fusion.31
  8.7 0.1 copy.14
  8.8 0.1 reduce-window.8
  8.9 0.1 add_reduce_fusion
  9.0 0.0 slice-start.2
  9.0 1.4 convolution_convert_fusion
  10.4 12.7 %all_gather.9 = bf16[128,3072]{1,0:T(8,128)(2,1)S(1)} all-gather(bf16[64,3072]{1,0:T(8,128)(2,1)S(1)} %convolution_convert_fusion), channel_id=1, replica_groups=mesh['dp'=2,'expert'=4,'mp'=4] {'dp'}, dimensions={0}, use_global_device_ids=true | all-gather | bytes 1179648 | tf_op jit(solution)/shard_map/all_gather | solution.py:25
  23.2 0.0 slice-start.3
  23.2 0.0 slice-start
  23.2 4.0 %fusion.4 = f32[128,1024]{1,0:T(8,128)S(1)} fusion(bf16[128,3072]{1,0:T(8,128)(2,1)S(1)} %all_gather.9, bf16[1,3072,1,1024]{3,1,2,0:T(8,128)(2,1)} %param.13), kind=kOutput, calls=%fused_computation.4 | convolution fusion | flops 805306368 | bytes 7602176 | tf_op jit(solution)/shard_map/dot_general | solution.py:26
  27.1 0.0 slice-done.2
  27.2 0.0 slice-done.3
  27.2 0.0 slice-start.1
  27.2 1.1 fusion.9
  28.3 8.2 %all_gather.10 = bf16[128,2048]{1,0:T(8,128)(2,1)S(1)} all-gather(bf16[128,1024]{1,0:T(8,128)(2,1)S(1)} %fusion.9), channel_id=1, replica_groups=mesh['dp'=2,'expert'=4,'mp'=4] {'dp'}, dimensions={1}, use_global_device_ids=true | all-gather | bytes 786432 | tf_op jit(solution)/shard_map/all_gather | solution.py:30
  36.4 0.0 slice-done
  36.4 0.0 slice-done.1
  36.4 0.0 copy-start.3
  36.4 0.0 copy-start.4
  36.5 1.0 fusion
  37.5 0.0 copy-start.1
  37.5 0.0 copy-start.2
  37.5 35.0 %all-reduce.6 = bf16[128,1536]{1,0:T(8,128)(2,1)} all-reduce(f32[128,1536]{1,0:T(8,128)S(1)} %fusion), channel_id=1, replica_groups=mesh['dp'=2,'expert'=4,'mp'=4] {'mp'}, use_global_device_ids=true, to_apply=%region_3.4 | all-reduce | flops 196608 | bytes 1179648 | tf_op jit(solution)/shard_map/psum | solution.py:34
  72.5 3.5 %all-to-all-start = ((bf16[2,64,1536]{2,1,0:T(8,128)(2,1)}), bf16[2,64,1536]{2,1,0:T(8,128)(2,1)S(1)}, u32[]{:S(2)}, u32[]{:S(2)}) async-start(bf16[2,64,1536]{2,1,0:T(8,128)(2,1)} %bitcast.4), calls=%async_computation | async-start | bytes 786432 | tf_op jit(solution)/shard_map/all_to_all | solution.py:35
  76.0 0.0 all-reduce.5.cloned.1.call-start
  76.0 0.0 copy-done.3
  76.1 0.0 copy-done.4
  76.1 5.8 %all-to-all-done = bf16[2,64,1536]{2,1,0:T(8,128)(2,1)S(1)} async-done(((bf16[2,64,1536]{2,1,0:T(8,128)(2,1)}), bf16[2,64,1536]{2,1,0:T(8,128)(2,1)S(1)}, u32[]{:S(2)}, u32[]{:S(2)}) %all-to-all-start) | async-done | bytes 393248 | tf_op jit(solution)/shard_map/all_to_all | solution.py:35
  81.9 1.4 fusion.19
  83.3 0.0 all-reduce.5.cloned.1.call-update
  83.3 0.0 all-gather.2.cloned.1.call-start
  83.4 0.5 all-gather.2.cloned.1.call-update
  83.9 32.0 %all-reduce.5.cloned.1.call-done = f32[64,3072]{1,0:T(8,128)} async-done(((f32[64,3072]{1,0:T(8,128)}), f32[64,3072]{1,0:T(8,128)}) %all-reduce.5.cloned.1.call-update) | async-done | bytes 786448 | tf_op jit(solution)/shard_map/psum | solution.py:43
  116.0 0.0 copy-done.1
  116.0 1.3 fusion.12
  117.3 0.0 copy-start
  117.3 118.1 %all-gather.2.cloned.1.call-done = bf16[3072,2048]{1,0:T(8,128)(2,1)} async-done(((bf16[1536,2048]{1,0:T(8,128)(2,1)}), bf16[3072,2048]{1,0:T(8,128)(2,1)}) %all-gather.2.cloned.1.call-update) | async-done | bytes 12582928 | tf_op jit(solution)/shard_map/all_gather | solution.py:54
  235.5 0.0 copy-done.2
  235.5 0.0 copy-start.5
  235.5 7.0 %fusion.32 = (f32[64]{0:T(128)S(1)}, f32[64,2048]{1,0:T(8,128)S(1)}) fusion(bf16[3072,2048]{1,0:T(8,128)(2,1)} %all-gather.2.cloned.1.call-done, bf16[64,3072]{1,0:T(8,128)(2,1)S(1)} %get-tuple-element.9, f32[3072]{0:T(1024)S(1)} %copy-done.2, f32[64]{0:T(128)S(1)} %add_rsqrt_fusion), kind=kOutput, calls=%fused_computation.39 | convolution fusion | flops 806223808 | bytes 13513216 | tf_op jit(solution)/shard_map/dot_general | solution.py:52
  242.5 0.0 copy-done
  242.5 33.2 %pmax.7 = f32[64]{0:T(128)S(1)} all-reduce(f32[64]{0:T(128)S(1)} %get-tuple-element.10), channel_id=1, replica_groups=mesh['dp'=2,'expert'=4,'mp'=4] {'expert','mp'}, use_global_device_ids=true, to_apply=%region_10.11 | all-reduce | flops 64 | bytes 512 | tf_op jit(solution)/shard_map/pmax | solution.py:61
  275.8 0.0 copy-done.5
  275.8 0.3 select_reduce_fusion
  276.0 8.4 %all-reduce = (f32[64]{0:T(128)S(1)}, f32[64]{0:T(128)S(1)}) all-reduce(f32[64]{0:T(128)S(1)} %get-tuple-element.3, f32[64]{0:T(128)S(1)} %get-tuple-element.2), channel_id=1, replica_groups=mesh['dp'=2,'expert'=4,'mp'=4] {'mp'}, use_global_device_ids=true, to_apply=%region_12.13 | all-reduce | flops 128 | bytes 1024 | tf_op jit(solution)/shard_map/psum | solution.py:63
  284.4 5.9 %all-reduce.1 = (f32[64]{0:T(128)S(1)}, f32[64]{0:T(128)S(1)}) all-reduce(f32[64]{0:T(128)S(1)} %get-tuple-element.4, f32[64]{0:T(128)S(1)} %get-tuple-element.5), channel_id=1, replica_groups=mesh['dp'=2,'expert'=4,'mp'=4] {'expert'}, use_global_device_ids=true, to_apply=%region_13.14 | all-reduce | flops 128 | bytes 1024 | tf_op jit(solution)/shard_map/psum | solution.py:63
  290.3 0.5 log_subtract_fusion
  (7 shorter events, 0.1 us)
Async XLA Ops:
  9.0 18.1 %slice-start.2 = ((s8[6291456]{0:T(1024)(128)(4,1)}), s8[4194304]{0:T(1024)(128)(4,1)S(1)}, s32[]{:S(2)}) async-start(s8[6291456]{0:T(1024)(128)(4,1)} %bitcast.29), calls=%async_computation.5 | async-start | bytes 8388608
  23.2 4.0 %slice-start.3 = ((s8[6291456]{0:T(1024)(128)(4,1)}), s8[2097152]{0:T(1024)(128)(4,1)S(1)}, s32[]{:S(2)}) async-start(s8[6291456]{0:T(1024)(128)(4,1)} %bitcast.29), calls=%async_computation.6 | async-start | bytes 4194304
  23.2 13.3 %slice-start = ((s8[6291456]{0:T(1024)(128)(4,1)}), s8[4194304]{0:T(1024)(128)(4,1)S(1)}, s32[]{:S(2)}) async-start(s8[6291456]{0:T(1024)(128)(4,1)} %bitcast.25), calls=%async_computation.3 | async-start | bytes 8388608
  27.2 9.3 %slice-start.1 = ((s8[6291456]{0:T(1024)(128)(4,1)}), s8[2097152]{0:T(1024)(128)(4,1)S(1)}, s32[]{:S(2)}) async-start(s8[6291456]{0:T(1024)(128)(4,1)} %bitcast.25), calls=%async_computation.4 | async-start | bytes 4194304
  36.4 39.6 %copy-start.3 = (s32[64,2]{0,1:T(2,128)S(1)}, s32[64,2]{0,1:T(2,128)}, u32[]{:S(2)}) copy-start(s32[64,2]{0,1:T(2,128)} %param.10) | copy-start | bytes 1540
  36.4 39.6 %copy-start.4 = (f32[64,2]{0,1:T(2,128)S(1)}, f32[64,2]{0,1:T(2,128)}, u32[]{:S(2)}) copy-start(f32[64,2]{0,1:T(2,128)} %param.11) | copy-start | bytes 1540
  37.5 78.5 %copy-start.1 = (bf16[64,3072]{1,0:T(8,128)(2,1)S(1)}, bf16[64,3072]{1,0:T(8,128)(2,1)}, u32[]{:S(2)}) copy-start(bf16[64,3072]{1,0:T(8,128)(2,1)} %param.9) | copy-start | bytes 1179652
  37.5 198.0 %copy-start.2 = (f32[3072]{0:T(1024)S(1)}, f32[3072]{0:T(1024)}, u32[]{:S(2)}) copy-start(f32[3072]{0:T(1024)} %param.16) | copy-start | bytes 36868
  72.5 9.3 %all-to-all-start = ((bf16[2,64,1536]{2,1,0:T(8,128)(2,1)}), bf16[2,64,1536]{2,1,0:T(8,128)(2,1)S(1)}, u32[]{:S(2)}, u32[]{:S(2)}) async-start(bf16[2,64,1536]{2,1,0:T(8,128)(2,1)} %bitcast.4), calls=%async_computation | async-start | bytes 786432 | tf_op jit(solution)/shard_map/all_to_all | solution.py:35
  76.0 40.0 %all-reduce.5.cloned.1.call-start = ((), (), s32[]{:S(2)}) async-start(), calls=%async_computation.1 | async-start | bytes 1572864 | tf_op jit(solution)/shard_map/psum | solution.py:43
  83.3 152.1 %all-gather.2.cloned.1.call-start = ((), (), s32[]{:S(2)}) async-start(), calls=%async_computation.2 | async-start | bytes 18874368 | tf_op jit(solution)/shard_map/all_gather | solution.py:54
  117.3 125.2 %copy-start = (bf16[64,3072]{1,0:T(8,128)(2,1)}, bf16[64,3072]{1,0:T(8,128)(2,1)S(1)}, u32[]{:S(2)}) copy-start(bf16[64,3072]{1,0:T(8,128)(2,1)S(1)} %get-tuple-element.9) | copy-start | bytes 1179652
  235.5 40.3 %copy-start.5 = (s32[64]{0:T(128)S(1)}, s32[64]{0:T(128)}, u32[]{:S(2)}) copy-start(s32[64]{0:T(128)} %param.12) | copy-start | bytes 772
Sparse Core Ops, SparseCore 0:
  83.4 32.4 all-reduce.4
Sparse Core Ops, SparseCore 1:
  85.4 150.0 all-gather.1
